TPU v7x, 512 devices: a whole 4x4x16 slice. The times are simulated.
512 devices in a mesh: space: 64 (over z_lo, x, core), batch: 8 (over z_hi, y).
Axes of the slice: x: 4, y: 4, z: 16 (z_hi: 2, z_lo: 8; z = z_hi * 8 + z_lo), core: 2. Of those that a mesh axis runs over, the one named last changes fastest.
Arguments:
- fine_parts: bfloat16 [8, 32768, 128], P('batch', 'space'), may hold values from -5 to 5
- parent_parts: bfloat16 [8, 4096, 128], P('batch', 'space'), may hold values from -5 to 5
- coarse_local: float32 [4096, 128], P('space'), may hold values from -6 to 6
- fine_source: int32 [189, 32768], P(None, 'space'), may hold values from 0 to 159
- fine_operator: int32 [189, 32768], P(None, 'space'), may hold values from 0 to 63
- parent_source: int32 [189, 4096], P(None, 'space'), may hold values from 0 to 159
- parent_operator: int32 [189, 4096], P(None, 'space'), may hold values from 0 to 63
- operators: bfloat16 [64, 128, 128], replicated, may hold values from -0.0390625 to 0.0390625
- child_shift: bfloat16 [8, 128, 128], replicated, may hold values from -0.5 to 0.5
- basis: bfloat16 [32768, 128, 128], P('space', 'batch'), may hold values from -0.5 to 0.5
- counts: int32 [8, 32768], P('batch', 'space'), may hold values from 1 to 16
Outputs:
- potential: float32 [128, 32768], P('batch', 'space')
Inputs may be any that keep to these rules, and one draw needn't show every extreme that they name: `fine_source`: an entry v names, in the target's own block if v // 32 is 0 and else in the block whose index differs from the target's in bit v // 32 - 1, box v % 32 of the aligned group of 32 boxes that holds the target's position. `parent_source`: an entry v names, in the target's own block if v // 32 is 0 and else in the block whose index differs from the target's in bit v // 32 - 1, parent box v % 32 of the aligned group of 32 parent boxes that holds the target's position.
All inputs are finite; a program needn't handle non-finite values.
Results may differ from a plain program's by a relative error of at most 0.015.
Values may be sent and summed in bfloat16 or wider, within the bound.
A program may use at most 64 MiB of HBM per device.

v0:
```python
import math

import jax
import jax.numpy as jnp
from jax import lax
from jax.sharding import PartitionSpec as P

NTERMS = 121
WINDOW = 32


def partner(shard, axis, apart):
    return lax.ppermute(shard, axis, [(i, i ^ 1 << apart) for i in range(lax.axis_size(axis))])


def far_field(stacked, source_list, operator_list, operators, row_start):
    kind_count, coef_width, _ = operators.shape
    flat_ops = operators.reshape(kind_count * coef_width, coef_width)
    list_length, total_rows = source_list.shape
    piece_rows = math.gcd(total_rows, WINDOW)
    piece_count = total_rows // piece_rows
    source_pieces = source_list.reshape(list_length, piece_count, piece_rows).transpose(1, 0, 2)
    kind_pieces = operator_list.reshape(list_length, piece_count, piece_rows).transpose(1, 0, 2)
    starts = row_start + lax.iota(jnp.int32, piece_count) * piece_rows
    kinds_iota = lax.iota(jnp.int32, kind_count)
    column_iota = lax.iota(jnp.int32, stacked.shape[0] * WINDOW)

    def one_piece(pieces):
        sources, kinds, start = pieces
        corner = start // WINDOW * WINDOW
        nearby = lax.dynamic_slice_in_dim(stacked, corner, WINDOW, 1).reshape(-1, coef_width)
        chosen = (sources[:, :, None] == column_iota).astype(jnp.bfloat16)
        onehot = (kinds[:, :, None] == kinds_iota).astype(jnp.bfloat16)
        counted = jnp.einsum(
            "jbt,jbr->btr", onehot, chosen, preferred_element_type=jnp.float32
        ).astype(jnp.bfloat16)
        grouped = jnp.einsum(
            "btr,rk->btk", counted, nearby, preferred_element_type=jnp.float32
        ).astype(jnp.bfloat16)
        return jnp.dot(
            grouped.reshape(piece_rows, kind_count * coef_width),
            flat_ops,
            preferred_element_type=jnp.float32,
        )

    return lax.map(one_piece, (source_pieces, kind_pieces, starts)).reshape(total_rows, coef_width)


def with_partners(fine_mult, parent_mult):
    fine_blocks = [fine_mult]
    parent_blocks = [parent_mult]
    for bit_number in range(4):
        fine_other, parent_other = partner((fine_mult, parent_mult), "space", bit_number)
        fine_blocks.append(fine_other)
        parent_blocks.append(parent_other)
    return (jnp.stack(fine_blocks), jnp.stack(parent_blocks))


def children(parent_local, fine_far, child_shift):
    shifted = jnp.einsum(
        "pk,okl->pol", parent_local, child_shift, preferred_element_type=jnp.float32
    )
    whole = shifted.reshape(fine_far.shape) + fine_far
    keep = lax.iota(jnp.int32, whole.shape[1]) < NTERMS
    return jnp.where(keep[None, :], whole, 0.0).astype(jnp.bfloat16)


def body(
    fine_parts,
    parent_parts,
    coarse_local,
    fine_source,
    fine_operator,
    parent_source,
    parent_operator,
    operators,
    child_shift,
    basis,
    counts,
):
    fine_terms = fine_parts[0].astype(jnp.float32)
    parent_terms = parent_parts[0].astype(jnp.float32)
    fine_total, parent_total = (
        lax.psum(fine_terms.astype(jnp.bfloat16), "batch").astype(jnp.float32),
        lax.psum(parent_terms.astype(jnp.bfloat16), "batch").astype(jnp.float32),
    )
    fine_stack, parent_stack = with_partners(
        fine_total.astype(jnp.bfloat16), parent_total.astype(jnp.bfloat16)
    )
    fine_far = far_field(fine_stack, fine_source, fine_operator, operators, 0)
    parent_far = far_field(parent_stack, parent_source, parent_operator, operators, 0)
    parent_local = (coarse_local + parent_far).astype(jnp.bfloat16)
    local = children(parent_local, fine_far, child_shift)
    values = lax.dot_general(
        basis, local, (((2,), (1,)), ((0,), (0,))), preferred_element_type=jnp.float32
    ).T
    slot_index = lax.iota(jnp.int32, values.shape[0])[:, None]
    return jnp.where(slot_index < counts, values, 0.0)


def solution(mesh):
    placed = (
        P("batch", "space", None),
        P("batch", "space", None),
        P("space", None),
        P(None, "space"),
        P(None, "space"),
        P(None, "space"),
        P(None, "space"),
        P(),
        P(),
        P("space", "batch", None),
        P("batch", "space"),
    )
    return jax.shard_map(
        body, mesh=mesh, in_specs=placed, out_specs=P("batch", "space"), check_vma=False
    )
```

profile of v0, /device:TPU:1, one launch (start us, length us, event | category | flops | bytes accessed | tf_op | source)
XLA Modules:
  0.0 527.7 jit_solution(15219592119479312412)
XLA Ops:
  6.5 75.3 %psum.14 = bf16[64,128]{1,0:T(8,128)(2,1)S(1)} all-reduce(bf16[64,128]{1,0:T(8,128)(2,1)} %bitcast.139), channel_id=1, replica_groups=mesh['space'=64,'batch'=8] {'batch'}, use_global_device_ids=true, to_apply=%region_0.0 | all-reduce | flops 8192 | bytes 32768 | tf_op jit(solution)/shard_map/psum | solution.py:85
  81.9 9.8 %collective-permute-start = (bf16[64,128]{1,0:T(8,128)(2,1)S(1)}, bf16[64,128]{1,0:T(8,128)(2,1)S(1)}, u32[]{:S(2)}, u32[]{:S(2)}) collective-permute-start(bf16[64,128]{1,0:T(8,128)(2,1)S(1)} %psum.14), channel_id=1, source_target_pairs={{0,8},{8,0},{16,24},{24,16},{32,40},{40,32},{48,56},{56,48},{64,72... | collective-permute-start | bytes 49160 | tf_op jit(solution)/shard_map/ppermute | solution.py:13
  91.7 3.1 collective-permute-start.1
  94.8 4.4 collective-permute-start.2
  99.2 2.6 collective-permute-start.3
  107.1 29.9 %while.26 = (s32[]{:T(128)}, f32[2,32,128]{2,1,0:T(8,128)}, s32[2,189,32]{1,2,0:T(8,128)}, s32[2,189,32]{1,2,0:T(8,128)}, s32[2]{0:T(128)}, /*index=5*/bf16[5,64...) while((s32[]{:T(128)}, f32[2,32,128]{2,1,0:T(8,128)}, ...), condition=%wide.region_2.3_spmd.clone, body=%wide.region_1.0_spmd.clone.sunk | while | flops 276802560 | bytes 6237277 | solution.py:46
  115.4 3.9 fusion.82
  119.3 2.8 fusion.83
  130.3 3.9 fusion.82
  134.2 2.8 fusion.83
  139.6 97.3 %all-reduce.2.cloned.1.call-done = bf16[512,128]{1,0:T(8,128)(2,1)} async-done(((bf16[512,128]{1,0:T(8,128)(2,1)}), bf16[512,128]{1,0:T(8,128)(2,1)}) %all-reduce.2.cloned.1.call-update) | async-done | bytes 131088 | tf_op jit(solution)/shard_map/psum | solution.py:84
  236.8 8.0 %collective-permute-start.4 = (bf16[512,128]{1,0:T(8,128)(2,1)}, bf16[512,128]{1,0:T(8,128)(2,1)S(1)}, u32[]{:S(2)}, u32[]{:S(2)}) collective-permute-start(bf16[512,128]{1,0:T(8,128)(2,1)} %all-reduce.2.cloned.1.call-done), channel_id=1, source_target_pairs={{0,8},{8,0},{16,24},{24,16},{32,40},{40,32},{48,56},{56,48},{64,72... | collective-permute-start | bytes 393224 | tf_op jit(solution)/shard_map/ppermute | solution.py:13
  244.9 3.1 collective-permute-start.5
  248.0 4.3 collective-permute-start.6
  259.6 258.1 %while.27 = (s32[]{:T(128)}, f32[16,32,128]{2,1,0:T(8,128)}, s32[16,189,32]{1,2,0:T(8,128)}, s32[16,189,32]{1,2,0:T(8,128)}, s32[16]{0:T(128)}, /*index=5*/bf16[...) while((s32[]{:T(128)}, f32[16,32,128]{2,1,0:T(8,128)}, ...), condition=%wide.region_5.6_spmd.clone, body=%wide.region_4.5_spmd.clone.sunk | while | flops 276802560 | bytes 6237277 | solution.py:46
  269.0 3.9 fusion.89
  272.9 2.7 fusion.90
  285.1 3.9 fusion.89
  289.1 2.7 fusion.90
  297.3 2.4 iota_compare_fusion.12
  301.3 3.9 fusion.89
  305.2 2.7 fusion.90
  317.4 3.9 fusion.89
  321.3 2.7 fusion.90
  333.5 3.9 fusion.89
  337.5 2.7 fusion.90
  349.7 3.9 fusion.89
  353.6 2.7 fusion.90
  365.8 3.9 fusion.89
  369.7 2.7 fusion.90
  381.9 3.9 fusion.89
  385.9 2.7 fusion.90
  398.1 3.9 fusion.89
  402.0 2.7 fusion.90
  414.2 3.9 fusion.89
  418.1 2.7 fusion.90
  430.3 3.9 fusion.89
  434.3 2.7 fusion.90
  446.5 3.9 fusion.89
  450.4 2.8 fusion.90
  462.6 3.9 fusion.89
  466.5 2.7 fusion.90
  478.7 3.9 fusion.89
  482.7 2.7 fusion.90
  494.9 3.9 fusion.89
  498.8 2.8 fusion.90
  511.0 3.9 fusion.89
  515.0 2.8 fusion.90
  (165 shorter events, 137.2 us)
Async XLA Ops:
  6.5 512.4 %copy-start = (bf16[512,16,128]{2,1,0:T(8,128)(2,1)S(1)}, bf16[512,16,128]{2,1,0:T(8,128)(2,1)}, u32[]{:S(2)}) copy-start(bf16[512,16,128]{2,1,0:T(8,128)(2,1)} %param.24) | copy-start | bytes 6291460
  6.5 230.3 %all-reduce.2.cloned.1.call-start = ((), (), s32[]{:S(2)}) async-start(), calls=%async_computation | async-start | bytes 262144 | tf_op jit(solution)/shard_map/psum | solution.py:84
  81.9 25.1 %collective-permute-start = (bf16[64,128]{1,0:T(8,128)(2,1)S(1)}, bf16[64,128]{1,0:T(8,128)(2,1)S(1)}, u32[]{:S(2)}, u32[]{:S(2)}) collective-permute-start(bf16[64,128]{1,0:T(8,128)(2,1)S(1)} %psum.14), channel_id=1, source_target_pairs={{0,8},{8,0},{16,24},{24,16},{32,40},{40,32},{48,56},{56,48},{64,72... | collective-permute-start | bytes 49160 | tf_op jit(solution)/shard_map/ppermute | solution.py:13
  91.7 15.3 %collective-permute-start.1 = (bf16[64,128]{1,0:T(8,128)(2,1)S(1)}, bf16[64,128]{1,0:T(8,128)(2,1)S(1)}, u32[]{:S(2)}, u32[]{:S(2)}) collective-permute-start(bf16[64,128]{1,0:T(8,128)(2,1)S(1)} %psum.14), channel_id=1, source_target_pairs={{0,16},{8,24},{16,0},{24,8},{32,48},{40,56},{48,32},{56,40},{64,80... | collective-permute-start | bytes 49160 | tf_op jit(solution)/shard_map/ppermute | solution.py:13
  94.8 12.2 %collective-permute-start.2 = (bf16[64,128]{1,0:T(8,128)(2,1)S(1)}, bf16[64,128]{1,0:T(8,128)(2,1)S(1)}, u32[]{:S(2)}, u32[]{:S(2)}) collective-permute-start(bf16[64,128]{1,0:T(8,128)(2,1)S(1)} %psum.14), channel_id=1, source_target_pairs={{0,32},{8,40},{16,48},{24,56},{32,0},{40,8},{48,16},{56,24},{64,96... | collective-permute-start | bytes 49160 | tf_op jit(solution)/shard_map/ppermute | solution.py:13
  99.2 7.9 %collective-permute-start.3 = (bf16[64,128]{1,0:T(8,128)(2,1)S(1)}, bf16[64,128]{1,0:T(8,128)(2,1)S(1)}, u32[]{:S(2)}, u32[]{:S(2)}) collective-permute-start(bf16[64,128]{1,0:T(8,128)(2,1)S(1)} %psum.14), channel_id=1, source_target_pairs={{0,64},{8,72},{16,80},{24,88},{32,96},{40,104},{48,112},{56,120},{... | collective-permute-start | bytes 49160 | tf_op jit(solution)/shard_map/ppermute | solution.py:13
  107.1 29.9 %copy-start.1 = (f32[64,128]{1,0:T(8,128)S(1)}, f32[64,128]{1,0:T(8,128)}, u32[]{:S(2)}) copy-start(f32[64,128]{1,0:T(8,128)} %param.17) | copy-start | bytes 98308
  236.8 19.3 %collective-permute-start.4 = (bf16[512,128]{1,0:T(8,128)(2,1)}, bf16[512,128]{1,0:T(8,128)(2,1)S(1)}, u32[]{:S(2)}, u32[]{:S(2)}) collective-permute-start(bf16[512,128]{1,0:T(8,128)(2,1)} %all-reduce.2.cloned.1.call-done), channel_id=1, source_target_pairs={{0,8},{8,0},{16,24},{24,16},{32,40},{40,32},{48,56},{56,48},{64,72... | collective-permute-start | bytes 393224 | tf_op jit(solution)/shard_map/ppermute | solution.py:13
  244.9 11.9 %collective-permute-start.5 = (bf16[512,128]{1,0:T(8,128)(2,1)}, bf16[512,128]{1,0:T(8,128)(2,1)S(1)}, u32[]{:S(2)}, u32[]{:S(2)}) collective-permute-start(bf16[512,128]{1,0:T(8,128)(2,1)} %all-reduce.2.cloned.1.call-done), channel_id=1, source_target_pairs={{0,16},{8,24},{16,0},{24,8},{32,48},{40,56},{48,32},{56,40},{64,80... | collective-permute-start | bytes 393224 | tf_op jit(solution)/shard_map/ppermute | solution.py:13
  248.0 9.5 %collective-permute-start.6 = (bf16[512,128]{1,0:T(8,128)(2,1)}, bf16[512,128]{1,0:T(8,128)(2,1)S(1)}, u32[]{:S(2)}, u32[]{:S(2)}) collective-permute-start(bf16[512,128]{1,0:T(8,128)(2,1)} %all-reduce.2.cloned.1.call-done), channel_id=1, source_target_pairs={{0,32},{8,40},{16,48},{24,56},{32,0},{40,8},{48,16},{56,24},{64,96... | collective-permute-start | bytes 393224 | tf_op jit(solution)/shard_map/ppermute | solution.py:13
  252.3 6.6 %collective-permute-start.7 = (bf16[512,128]{1,0:T(8,128)(2,1)}, bf16[512,128]{1,0:T(8,128)(2,1)S(1)}, u32[]{:S(2)}, u32[]{:S(2)}) collective-permute-start(bf16[512,128]{1,0:T(8,128)(2,1)} %all-reduce.2.cloned.1.call-done), channel_id=1, source_target_pairs={{0,64},{8,72},{16,80},{24,88},{32,96},{40,104},{48,112},{56,120},{... | collective-permute-start | bytes 393224 | tf_op jit(solution)/shard_map/ppermute | solution.py:13
  517.7 2.5 copy-start.2
Sparse Core Ops, SparseCore 0:
  102.0 134.8 all-reduce.1
where the time goes:
time: 532 us; the launch traced here: 528 us
  matrix products  123 us (23%)
  waiting for transfers between devices  98 us (18%)
  blocking collectives  75.3 us (14%)
  other arithmetic  72.8 us (14%)
  local copies, waits for them, and re-layouts  60.8 us (11%)
  loops' own time  46.5 us (9%)
  starting transfers between devices  37.6 us (7%)
  between operations  13.5 us (3%)
    psum x1, waiting for transfers between devices, body(): lax.psum(fine_terms.astype(jnp.bfloat16), 'batch').astype(jnp.float32)  97.3 us
    psum x1, blocking collectives, body(): lax.psum(parent_terms.astype(jnp.bfloat16), 'batch').astype(jnp.float32)  75.3 us
    dot_general x18, matrix products, one_piece(): jnp.einsum('btr,rk->btk', counted, nearby, preferred_element_type=jnp.flo...  70.7 us
    dot_general x18, matrix products, one_piece(): jnp.dot(grouped.reshape(piece_rows, kind_count * coef_width), flat_ops, p...  49.5 us
    another operation x2, loops' own time, far_field(): lax.map(one_piece, (source_pieces, kind_pieces, starts))  46.5 us
    eq x18, other arithmetic, one_piece(): chosen = (sources[:, :, None] == column_iota).astype(jnp.bfloat16)  42.6 us
    dynamic_slice x72, local copies, waits for them, and re-layouts, far_field(): lax.map(one_piece, (source_pieces, kind_pieces, starts))  39.7 us
    ppermute x8, starting transfers between devices, partner(): lax.ppermute(shard, axis, [(i, i ^ 1 << apart) for i in range(lax.axis_si...  37.6 us
  transfers between devices with their start and end apart: 9, of which 2 were waited for; matrix products, arithmetic and copies ran while one was open for 7% of the time, Pallas kernels for 0%

commit v1 on v0

v1 whole, which is shorter than its diff:
```python
import functools

import jax
import jax.numpy as jnp
from jax import lax
from jax.experimental import pallas as pl
from jax.experimental.pallas import tpu as pltpu
from jax.sharding import PartitionSpec as P

NTERMS = 121
NI = 189
NC = 128
NOPS = 64
WINDOW = 32
REACH = 5 * WINDOW
ROWS = 128
PROWS = 16
WINDOWS = ROWS // WINDOW
MESH = pl.DeviceIdType.MESH
F32 = jnp.float32
BF16 = jnp.bfloat16


def remote(src, dst, send_sem, recv_sem, device):
    return pltpu.make_async_remote_copy(
        src_ref=src,
        dst_ref=dst,
        send_sem=send_sem,
        recv_sem=recv_sem,
        device_id=device,
        device_id_type=MESH,
    )


def greet(devices):
    barrier = pltpu.get_barrier_semaphore()
    for device in devices:
        pl.semaphore_signal(barrier, inc=1, device_id=device, device_id_type=MESH)


def await_greetings(devices):
    pl.semaphore_wait(pltpu.get_barrier_semaphore(), len(devices))


def one_box(source_row, kind_row, iota_ref):
    source = jnp.broadcast_to(source_row, (16, 256)).astype(BF16)
    kind = jnp.broadcast_to(kind_row, (16, 256)).astype(BF16)
    one, none = jnp.ones((), BF16), jnp.zeros((), BF16)
    iota = iota_ref[...]
    sources = jnp.concatenate([source] * (REACH // 16), axis=0)
    kinds = jnp.concatenate([kind] * (NOPS // 16), axis=0)
    chosen = jnp.where(sources == iota, one, none)
    onehot = jnp.where(kinds == iota[:NOPS], one, none)
    counted = lax.dot_general(
        onehot, chosen, (((1,), (1,)), ((), ())), preferred_element_type=F32
    )
    return jnp.concatenate([counted, jnp.zeros((NOPS, 256 - REACH), F32)], axis=1)


def lists_across(source_v, kind_v):
    entry = lax.broadcasted_iota(jnp.int32, (256, 1), 0)
    source = jnp.where(entry < NI, source_v[...], 255).astype(F32)
    kind = jnp.where(entry < NI, kind_v[...], 255).astype(F32)
    return source.T, kind.T


def kernel(
    fine_parts,
    parent_parts,
    coarse,
    fine_source,
    fine_operator,
    parent_source,
    parent_operator,
    operators,
    child_shift,
    basis,
    out,
    source_v,
    kind_v,
    psource_v,
    pkind_v,
    source_t,
    kind_t,
    psource_t,
    pkind_t,
    iota_v,
    own_v,
    coarse_v,
    ops_v,
    shift_v,
    basis_v,
    counted_f,
    counted_v,
    pcounted_v,
    from_y,
    half_v,
    from_z,
    near_v,
    grouped_v,
    spread_v,
    local_v,
    load_sem,
    y_send,
    y_recv,
    z_send,
    z_recv,
    n_send,
    n_recv,
    l_send,
    l_recv,
):
    d = lax.axis_index("space")
    i = lax.axis_index("batch")
    h, y = i // 4, i % 4
    y_peers = [(d, h * 4 + (y + o) % 4) for o in (1, 2, 3)]
    z_peer = (d, (1 - h) * 4 + y)
    partners = [(d + (1 - 2 * ((d // s) % 2)) * s, i) for s in (1, 2, 4, 8)]
    everyone = y_peers + [z_peer] + partners
    greet(everyone)

    def load(src, dst, n):
        copy = pltpu.make_async_copy(src, dst, load_sem.at[n])
        copy.start()
        return copy

    row0 = pl.multiple_of(y * ROWS, ROWS)
    prow0 = pl.multiple_of(y * PROWS, PROWS)
    pwin0 = pl.multiple_of((y // 2) * WINDOW, WINDOW)
    lists = [
        load(parent_source, psource_v.at[pl.ds(0, NI)], 0),
        load(parent_operator, pkind_v.at[pl.ds(0, NI)], 1),
        load(fine_source.at[:, pl.ds(row0, ROWS)], source_v.at[pl.ds(0, NI)], 2),
        load(fine_operator.at[:, pl.ds(row0, ROWS)], kind_v.at[pl.ds(0, NI)], 3),
    ]
    mine = [
        load(fine_parts.at[0, pl.ds(row0, ROWS)], own_v.at[pl.ds(0, ROWS)], 4),
        load(parent_parts.at[0, pl.ds(pwin0, WINDOW)], own_v.at[pl.ds(ROWS, WINDOW)], 5),
        load(coarse.at[pl.ds(prow0, PROWS)], coarse_v, 6),
    ]
    weights = [
        load(operators, ops_v, 7),
        load(child_shift, shift_v, 8),
        load(basis, basis_v, 9),
    ]

    iota_v[...] = lax.broadcasted_iota(jnp.int32, (REACH, 256), 0).astype(F32).astype(BF16)
    for copy in lists:
        copy.wait()
    psource_t[...], pkind_t[...] = lists_across(psource_v, pkind_v)
    source_t[...], kind_t[...] = lists_across(source_v, kind_v)

    def count_into(source_ref, kind_ref, start, boxes, target):
        def few(step, carry):
            for k in range(4):
                b = step * 4 + k
                counted = one_box(
                    source_ref[pl.ds(start + b, 1), :], kind_ref[pl.ds(start + b, 1), :], iota_v
                )
                counted_f[0, pl.ds(b, NOPS, stride=boxes), :] = counted[:, :128]
                counted_f[1, pl.ds(b, NOPS, stride=boxes), :] = counted[:, 128:]
            return carry

        lax.fori_loop(0, boxes // 4, few, 0)

        def narrow(step, carry):
            rows = pl.ds(pl.multiple_of(step * 256, 256), 256)
            target[rows, 0:128] = counted_f[0, rows, :].astype(BF16)
            target[rows, 128:256] = counted_f[1, rows, :].astype(BF16)
            return carry

        lax.fori_loop(0, NOPS * boxes // 256, narrow, 0)

    def count_windows(first, last):
        def window(w, carry):
            count_into(source_t, kind_t, w * WINDOW, WINDOW, counted_v.at[w])
            return carry

        lax.fori_loop(first, last, window, 0)

    count_into(psource_t, pkind_t, prow0, PROWS, pcounted_v)

    await_greetings(everyone)
    sends = []
    y_copies = []
    for o, device in enumerate(y_peers):
        there = (y + o + 1) % 4
        theirs = pl.multiple_of(there * ROWS, ROWS)
        theirs_p = pl.multiple_of((there // 2) * WINDOW, WINDOW)
        y_copies.append(
            remote(
                fine_parts.at[0, pl.ds(theirs, ROWS)],
                from_y.at[o, pl.ds(0, ROWS)],
                y_send.at[2 * o],
                y_recv.at[2 * o],
                device,
            )
        )
        y_copies.append(
            remote(
                parent_parts.at[0, pl.ds(theirs_p, WINDOW)],
                from_y.at[o, pl.ds(ROWS, WINDOW)],
                y_send.at[2 * o + 1],
                y_recv.at[2 * o + 1],
                device,
            )
        )
    for copy in y_copies:
        copy.start()
    sends += y_copies

    count_windows(0, 1)
    for copy in mine:
        copy.wait()
    for copy in y_copies:
        copy.wait_recv()
    half = own_v[...].astype(F32)
    for o in range(3):
        half = half + from_y[o].astype(F32)
    half_v[...] = half.astype(BF16)

    z_copy = remote(half_v, from_z, z_send, z_recv, z_peer)
    z_copy.start()
    sends.append(z_copy)
    count_windows(1, 3)
    z_copy.wait_recv()
    near_v[0] = (half_v[...].astype(F32) + from_z[...].astype(F32)).astype(BF16)

    n_copies = [
        remote(near_v.at[0], near_v.at[k + 1], n_send.at[k], n_recv.at[k], device)
        for k, device in enumerate(partners)
    ]
    for copy in n_copies:
        copy.start()
    sends += n_copies
    count_windows(3, 4)
    for copy in weights:
        copy.wait()
    for copy in n_copies:
        copy.wait_recv()

    nothing = jnp.zeros((256 - REACH, NC), BF16)
    for w in range(WINDOWS + 1):
        fine = w < WINDOWS
        boxes = WINDOW if fine else PROWS
        near = near_v[:, w * WINDOW : (w + 1) * WINDOW, :].reshape(REACH, NC)
        near = jnp.concatenate([near, nothing], axis=0)
        counted = counted_v.at[w] if fine else pcounted_v
        kinds = 512 // boxes
        for c in range(NOPS // kinds):
            grouped = jnp.dot(
                counted[c * 512 : (c + 1) * 512, :], near, preferred_element_type=F32
            ).astype(BF16)
            for t in range(kinds):
                kind = c * kinds + t
                grouped_v[
                    w * WINDOW : w * WINDOW + boxes, kind * NC : (kind + 1) * NC
                ] = grouped[t * boxes : (t + 1) * boxes, :]
    far = jnp.dot(
        grouped_v[...], ops_v[...].reshape(NOPS * NC, NC), preferred_element_type=F32
    )
    parent_local = (coarse_v[...] + far[ROWS:, :]).astype(BF16)
    for octant in range(8):
        spread_v[pl.ds(octant, PROWS, stride=8), :] = jnp.dot(
            parent_local, shift_v[octant], preferred_element_type=F32
        )
    keep = lax.broadcasted_iota(jnp.int32, (ROWS, NC), 1) < NTERMS
    local_v[pl.ds(row0, ROWS), :] = jnp.where(keep, spread_v[...] + far[:ROWS, :], 0.0).astype(BF16)

    l_copies = [
        remote(
            local_v.at[pl.ds(row0, ROWS)],
            local_v.at[pl.ds(row0, ROWS)],
            l_send.at[o],
            l_recv.at[o],
            device,
        )
        for o, device in enumerate(y_peers)
    ]
    for copy in l_copies:
        copy.start()
    sends += l_copies

    lane = lax.broadcasted_iota(jnp.int32, (16, ROWS), 1)

    def evaluate(start):
        local = local_v[pl.ds(start, ROWS), :]
        found = jnp.zeros((16, ROWS), F32)
        for c in range(ROWS // 32):
            slots = basis_v[pl.ds(start + c * 32, 32)].reshape(32 * 16, NC)
            values = lax.dot_general(
                slots, local, (((1,), (1,)), ((), ())), preferred_element_type=F32
            )
            for b in range(32):
                found = jnp.where(lane == c * 32 + b, values[b * 16 : (b + 1) * 16, :], found)
        out[:, pl.ds(start, ROWS)] = found

    evaluate(row0)
    for o, copy in enumerate(l_copies):
        copy.wait_recv()
        evaluate(pl.multiple_of(((y + 3 - o) % 4) * ROWS, ROWS))
    for copy in sends:
        copy.wait_send()


def body(
    fine_parts,
    parent_parts,
    coarse_local,
    fine_source,
    fine_operator,
    parent_source,
    parent_operator,
    operators,
    child_shift,
    basis,
    counts,
):
    boxes, slots, _ = basis.shape
    parents = coarse_local.shape[0]
    vmem = pltpu.VMEM
    dma = pltpu.SemaphoreType.DMA
    message = ROWS + WINDOW
    values = pl.pallas_call(
        kernel,
        out_shape=jax.ShapeDtypeStruct((slots, boxes), F32),
        in_specs=[pl.BlockSpec(memory_space=pl.ANY)] * 10,
        out_specs=pl.BlockSpec(memory_space=pltpu.VMEM),
        scratch_shapes=[
            vmem((256, ROWS), jnp.int32),
            vmem((256, ROWS), jnp.int32),
            vmem((256, parents), jnp.int32),
            vmem((256, parents), jnp.int32),
            vmem((ROWS, 256), F32),
            vmem((ROWS, 256), F32),
            vmem((parents, 256), F32),
            vmem((parents, 256), F32),
            vmem((REACH, 256), BF16),
            vmem((message, NC), BF16),
            vmem((PROWS, NC), F32),
            vmem((NOPS, NC, NC), BF16),
            vmem((8, NC, NC), BF16),
            vmem((boxes, slots, NC), BF16),
            vmem((2, NOPS * WINDOW, 128), F32),
            vmem((WINDOWS, NOPS * WINDOW, 256), BF16),
            vmem((NOPS * PROWS, 256), BF16),
            vmem((3, message, NC), BF16),
            vmem((message, NC), BF16),
            vmem((message, NC), BF16),
            vmem((5, message, NC), BF16),
            vmem((ROWS + PROWS, NOPS * NC), BF16),
            vmem((ROWS, NC), F32),
            vmem((boxes, NC), BF16),
            dma((10,)),
            dma((6,)),
            dma((6,)),
            dma,
            dma,
            dma((4,)),
            dma((4,)),
            dma((3,)),
            dma((3,)),
        ],
        compiler_params=pltpu.CompilerParams(
            collective_id=0, has_side_effects=True, vmem_limit_bytes=40 * 1024 * 1024
        ),
    )(
        fine_parts,
        parent_parts,
        coarse_local,
        fine_source,
        fine_operator,
        parent_source,
        parent_operator,
        operators,
        child_shift,
        basis,
    )
    slot_index = lax.iota(jnp.int32, slots)[:, None]
    return jnp.where(slot_index < counts, values, 0.0)


def solution(mesh):
    placed = (
        P("batch", "space", None),
        P("batch", "space", None),
        P("space", None),
        P(None, "space"),
        P(None, "space"),
        P(None, "space"),
        P(None, "space"),
        P(),
        P(),
        P("space", "batch", None),
        P("batch", "space"),
    )
    return jax.shard_map(
        body, mesh=mesh, in_specs=placed, out_specs=P("batch", "space"), check_vma=False
    )
```

time: 532 us -> 49.8 us (0.09)
  the two profiles are of different devices: /device:TPU:1 before, /device:TPU:8 now
where the time goes in v1:
time: 49.8 us; the launch traced here: 49.2 us
  Pallas kernels  38.2 us (77%)
  local copies, waits for them, and re-layouts  10.4 us (21%)
  other arithmetic  0.62 us (1%)
    pallas_call x1, Pallas kernels, body(): pl.pallas_call(kernel, out_shape=jax.ShapeDtypeStruct((slots, boxes), F32...  38.2 us
    unnamed x20, local copies, waits for them, and re-layouts  10.4 us

profile of v1, /device:TPU:8, one launch (start us, length us, event | category | flops | bytes accessed | tf_op | source)
XLA Modules:
  0.0 49.2 jit_solution(10684795593466114148)
XLA Ops:
  0.0 0.9 %copy.12.parent_source = s32[189,64]{1,0:T(8,128)S(1)} copy(s32[189,64]{0,1:T(8,128)} %param.16) | data formatting | bytes 96768 | tf_op args[5]
  0.9 0.9 %copy.13.parent_operator = s32[189,64]{1,0:T(8,128)S(1)} copy(s32[189,64]{0,1:T(8,128)} %param.17) | data formatting | bytes 96768 | tf_op args[6]
  1.9 0.0 copy-start
  1.9 1.6 %copy-done = bf16[64,128,128]{2,1,0:T(8,128)(2,1)S(1)} copy-done((bf16[64,128,128]{2,1,0:T(8,128)(2,1)S(1)}, bf16[64,128,128]{2,1,0:T(8,128)(2,1)}, u32[]{:S(2)}) %copy-start) | copy-done | bytes 2097176
  3.5 0.0 copy-start.1
  3.5 1.6 %copy-done.1 = bf16[512,16,128]{2,1,0:T(8,128)(2,1)S(1)} copy-done((bf16[512,16,128]{2,1,0:T(8,128)(2,1)S(1)}, bf16[512,16,128]{2,1,0:T(8,128)(2,1)}, u32[]{:S(2)}) %copy-start.1) | copy-done | bytes 2097176
  5.1 0.0 copy-start.2
  5.1 1.0 %copy-done.2 = s32[189,512]{1,0:T(8,128)S(1)} copy-done((s32[189,512]{1,0:T(8,128)S(1)}, s32[189,512]{1,0:T(8,128)}, u32[]{:S(2)}) %copy-start.2) | copy-done | bytes 387096
  6.1 0.0 copy-start.3
  6.1 1.0 %copy-done.3 = s32[189,512]{1,0:T(8,128)S(1)} copy-done((s32[189,512]{1,0:T(8,128)S(1)}, s32[189,512]{1,0:T(8,128)}, u32[]{:S(2)}) %copy-start.3) | copy-done | bytes 387096
  7.1 0.0 copy-start.4
  7.1 0.9 %copy-done.4 = bf16[8,128,128]{2,1,0:T(8,128)(2,1)S(1)} copy-done((bf16[8,128,128]{2,1,0:T(8,128)(2,1)S(1)}, bf16[8,128,128]{2,1,0:T(8,128)(2,1)}, u32[]{:S(2)}) %copy-start.4) | copy-done | bytes 262168
  8.0 0.0 copy-start.5
  8.0 0.9 %copy-done.5 = bf16[1,512,128]{2,1,0:T(8,128)(2,1)S(1)} copy-done((bf16[1,512,128]{2,1,0:T(8,128)(2,1)S(1)}, bf16[1,512,128]{2,1,0:T(8,128)(2,1)}, u32[]{:S(2)}) %copy-start.5) | copy-done | bytes 131096
  8.9 0.0 copy-start.6
  8.9 0.8 %copy-done.6 = f32[64,128]{1,0:T(8,128)S(1)} copy-done((f32[64,128]{1,0:T(8,128)S(1)}, f32[64,128]{1,0:T(8,128)}, u32[]{:S(2)}) %copy-start.6) | copy-done | bytes 32792
  9.7 0.0 copy-start.7
  9.7 0.7 %copy-done.7 = bf16[1,64,128]{2,1,0:T(8,128)(2,1)S(1)} copy-done((bf16[1,64,128]{2,1,0:T(8,128)(2,1)S(1)}, bf16[1,64,128]{2,1,0:T(8,128)(2,1)}, u32[]{:S(2)}) %copy-start.7) | copy-done | bytes 16408
  10.4 0.0 copy-start.8
  10.4 38.2 %shard_map.109 = f32[16,512]{1,0:T(8,128)S(1)} custom-call(bf16[1,512,128]{2,1,0:T(8,128)(2,1)S(1)} %copy-done.5, bf16[1,64,128]{2,1,0:T(8,128)(2,1)S(1)} %copy-done.7, f32[64,128]{1,0:T(8,128)S(1)} %copy-done.6, s32[189,512]{1,0:T(8,128)S(1)} %copy-done.2, s32[189,512]{1,0:T(8,128)S(1)} %copy-done.3, s32[189,64]{1,0:T(8,128)S(1)} %copy.12.parent_source, ...), custom_call_target="tpu_custom_call" | custom-call | tf_op jit(solution)/shard_map/pallas_call | solution.py:324
  48.6 0.0 copy-done.8
  48.6 0.6 %fusion = f32[16,512]{1,0:T(8,128)} fusion(f32[16,512]{1,0:T(8,128)S(1)} %shard_map.109, s32[512]{0:T(512)S(1)} %bitcast.1), kind=kLoop, calls=%fused_computation.1 | loop fusion | flops 16384 | bytes 67584 | tf_op jit(solution)/shard_map/jit(_where)/select_n | solution.py:380
Async XLA Ops:
  1.9 1.6 %copy-start = (bf16[64,128,128]{2,1,0:T(8,128)(2,1)S(1)}, bf16[64,128,128]{2,1,0:T(8,128)(2,1)}, u32[]{:S(2)}) copy-start(bf16[64,128,128]{2,1,0:T(8,128)(2,1)} %operators.1) | copy-start | bytes 6291460
  3.5 1.6 %copy-start.1 = (bf16[512,16,128]{2,1,0:T(8,128)(2,1)S(1)}, bf16[512,16,128]{2,1,0:T(8,128)(2,1)}, u32[]{:S(2)}) copy-start(bf16[512,16,128]{2,1,0:T(8,128)(2,1)} %basis.1) | copy-start | bytes 6291460
  5.1 1.0 %copy-start.2 = (s32[189,512]{1,0:T(8,128)S(1)}, s32[189,512]{1,0:T(8,128)}, u32[]{:S(2)}) copy-start(s32[189,512]{1,0:T(8,128)} %fine_source.1) | copy-start | bytes 1161220
  6.1 1.0 %copy-start.3 = (s32[189,512]{1,0:T(8,128)S(1)}, s32[189,512]{1,0:T(8,128)}, u32[]{:S(2)}) copy-start(s32[189,512]{1,0:T(8,128)} %fine_operator.1) | copy-start | bytes 1161220
  7.1 0.9 %copy-start.4 = (bf16[8,128,128]{2,1,0:T(8,128)(2,1)S(1)}, bf16[8,128,128]{2,1,0:T(8,128)(2,1)}, u32[]{:S(2)}) copy-start(bf16[8,128,128]{2,1,0:T(8,128)(2,1)} %child_shift.1) | copy-start | bytes 786436
  8.0 0.9 %copy-start.5 = (bf16[1,512,128]{2,1,0:T(8,128)(2,1)S(1)}, bf16[1,512,128]{2,1,0:T(8,128)(2,1)}, u32[]{:S(2)}) copy-start(bf16[1,512,128]{2,1,0:T(8,128)(2,1)} %fine_parts.1) | copy-start | bytes 393220
  8.9 0.8 %copy-start.6 = (f32[64,128]{1,0:T(8,128)S(1)}, f32[64,128]{1,0:T(8,128)}, u32[]{:S(2)}) copy-start(f32[64,128]{1,0:T(8,128)} %coarse.1) | copy-start | bytes 98308
  9.7 0.7 %copy-start.7 = (bf16[1,64,128]{2,1,0:T(8,128)(2,1)S(1)}, bf16[1,64,128]{2,1,0:T(8,128)(2,1)}, u32[]{:S(2)}) copy-start(bf16[1,64,128]{2,1,0:T(8,128)(2,1)} %parent_parts.1) | copy-start | bytes 49156
  10.4 38.2 %copy-start.8 = (s32[1,512]{1,0:T(1,128)S(1)}, s32[1,512]{1,0:T(1,128)}, u32[]{:S(2)}) copy-start(s32[1,512]{1,0:T(1,128)} %param.21) | copy-start | bytes 6148

commit v2 on v1

v2 whole, which is shorter than its diff:
```python
import functools

import jax
import jax.numpy as jnp
from jax import lax
from jax.experimental import pallas as pl
from jax.experimental.pallas import tpu as pltpu
from jax.sharding import PartitionSpec as P

NTERMS = 121
NI = 189
NC = 128
NOPS = 64
WINDOW = 32
REACH = 5 * WINDOW
ROWS = 128
PROWS = 16
WINDOWS = ROWS // WINDOW
MESSAGE = WINDOW + ROWS
FIRST = 3 * WINDOW
PIECES = ((slice(0, FIRST), (0, 1)), (slice(FIRST, MESSAGE), (2,)))
MESH = pl.DeviceIdType.MESH
F32 = jnp.float32
BF16 = jnp.bfloat16


def remote(src, dst, send_sem, recv_sem, device):
    return pltpu.make_async_remote_copy(
        src_ref=src,
        dst_ref=dst,
        send_sem=send_sem,
        recv_sem=recv_sem,
        device_id=device,
        device_id_type=MESH,
    )


def greet(devices):
    barrier = pltpu.get_barrier_semaphore()
    for device in devices:
        pl.semaphore_signal(barrier, inc=1, device_id=device, device_id_type=MESH)


def await_greetings(devices):
    pl.semaphore_wait(pltpu.get_barrier_semaphore(), len(devices))


def one_box(source_row, kind_row, iota_ref):
    source = jnp.broadcast_to(source_row, (16, 256)).astype(BF16)
    kind = jnp.broadcast_to(kind_row, (16, 256)).astype(BF16)
    one, none = jnp.ones((), BF16), jnp.zeros((), BF16)
    iota = iota_ref[...]
    sources = jnp.concatenate([source] * (REACH // 16), axis=0)
    kinds = jnp.concatenate([kind] * (NOPS // 16), axis=0)
    chosen = jnp.where(sources == iota, one, none)
    onehot = jnp.where(kinds == iota[:NOPS], one, none)
    counted = lax.dot_general(
        onehot, chosen, (((1,), (1,)), ((), ())), preferred_element_type=F32
    )
    return jnp.concatenate([counted, jnp.zeros((NOPS, 256 - REACH), F32)], axis=1)


def lists_across(source_v, kind_v):
    entry = lax.broadcasted_iota(jnp.int32, (256, 1), 0)
    source = jnp.where(entry < NI, source_v[...], 255).astype(F32)
    kind = jnp.where(entry < NI, kind_v[...], 255).astype(F32)
    return source.T, kind.T


def kernel(
    fine_parts,
    parent_parts,
    coarse,
    fine_source,
    fine_operator,
    parent_source,
    parent_operator,
    operators,
    child_shift,
    basis,
    out,
    source_v,
    kind_v,
    psource_v,
    pkind_v,
    source_t,
    kind_t,
    psource_t,
    pkind_t,
    iota_v,
    own_v,
    coarse_v,
    ops_v,
    shift_v,
    basis_v,
    counted_f,
    counted_v,
    pcounted_v,
    from_y,
    half_v,
    from_z,
    near_v,
    grouped_v,
    spread_v,
    local_v,
    load_sem,
    y_send,
    y_recv,
    z_send,
    z_recv,
    n_send,
    n_recv,
    l_send,
    l_recv,
):
    d = lax.axis_index("space")
    i = lax.axis_index("batch")
    h, y = i // 4, i % 4
    y_peers = [(d, h * 4 + (y + o) % 4) for o in (1, 2, 3)]
    z_peer = (d, (1 - h) * 4 + y)
    partners = [(d + (1 - 2 * ((d // s) % 2)) * s, i) for s in (4, 8, 2, 1)]
    blocks = (3, 4, 2, 1)
    everyone = y_peers + [z_peer] + partners
    greet(everyone)

    def load(src, dst, n):
        copy = pltpu.make_async_copy(src, dst, load_sem.at[n])
        copy.start()
        return copy

    row0 = pl.multiple_of(y * ROWS, ROWS)
    prow0 = pl.multiple_of(y * PROWS, PROWS)
    pwin0 = pl.multiple_of((y // 2) * WINDOW, WINDOW)
    mine = [
        load(parent_parts.at[0, pl.ds(pwin0, WINDOW)], own_v.at[pl.ds(0, WINDOW)], 4),
        load(fine_parts.at[0, pl.ds(row0, ROWS)], own_v.at[pl.ds(WINDOW, ROWS)], 5),
    ]
    lists = [
        load(fine_source.at[:, pl.ds(row0, ROWS)], source_v.at[pl.ds(0, NI)], 0),
        load(fine_operator.at[:, pl.ds(row0, ROWS)], kind_v.at[pl.ds(0, NI)], 1),
        load(parent_source.at[pl.ds(prow0, PROWS)], psource_v, 2),
        load(parent_operator.at[pl.ds(prow0, PROWS)], pkind_v, 3),
    ]

    def count_into(source_ref, kind_ref, start, boxes, target):
        for b in range(boxes):
            counted = one_box(
                source_ref[pl.ds(start + b, 1), :], kind_ref[pl.ds(start + b, 1), :], iota_v
            )
            counted_f[0, pl.ds(b, NOPS, stride=boxes + 1), :] = counted[:, :128]
            counted_f[1, pl.ds(b, NOPS, stride=boxes + 1), :] = counted[:, 128:]

        def narrow(step, carry):
            for k in range(8):
                kind = step * 8 + k
                rows = pl.ds(pl.multiple_of(kind * boxes, boxes), boxes)
                wide = pl.ds(kind * (boxes + 1), boxes)
                target[rows, 0:128] = counted_f[0, wide, :].astype(BF16)
                target[rows, 128:256] = counted_f[1, wide, :].astype(BF16)
            return carry

        lax.fori_loop(0, NOPS // 8, narrow, 0)

    def count_windows(first, last):
        def window(w, carry):
            count_into(source_t, kind_t, w * WINDOW, WINDOW, counted_v.at[w])
            return carry

        lax.fori_loop(first, last, window, 0)

    await_greetings(everyone)
    y_copies = []
    for o, device in enumerate(y_peers):
        there = (y + o + 1) % 4
        theirs = pl.multiple_of(there * ROWS, ROWS)
        theirs_p = pl.multiple_of((there // 2) * WINDOW, WINDOW)
        parts = (
            (parent_parts.at[0, pl.ds(theirs_p, WINDOW)], 0, WINDOW),
            (fine_parts.at[0, pl.ds(theirs, FIRST - WINDOW)], WINDOW, FIRST - WINDOW),
            (
                fine_parts.at[0, pl.ds(theirs + FIRST - WINDOW, MESSAGE - FIRST)],
                FIRST,
                MESSAGE - FIRST,
            ),
        )
        y_copies.append(
            [
                remote(
                    src,
                    from_y.at[o, pl.ds(at, rows)],
                    y_send.at[o * 3 + n],
                    y_recv.at[o * 3 + n],
                    device,
                )
                for n, (src, at, rows) in enumerate(parts)
            ]
        )
    for n in range(3):
        for o in (1, 0, 2):
            y_copies[o][n].start()
    weights = [
        load(coarse.at[pl.ds(prow0, PROWS)], coarse_v, 6),
        load(operators, ops_v, 7),
        load(child_shift, shift_v, 8),
        load(basis, basis_v, 9),
    ]
    sends = [copy for copies in y_copies for copy in copies]

    iota_v[...] = lax.broadcasted_iota(jnp.int32, (REACH, 256), 0).astype(F32).astype(BF16)
    for copy in lists:
        copy.wait()
    for lists_v, across in ((psource_v, psource_t), (pkind_v, pkind_t)):
        across[:, 128:256] = jnp.full((PROWS, 128), 255.0, F32)
        across[:, 0:128] = lists_v[:, 0:128].astype(F32)
        across[:, 128:NI] = lists_v[:, 128:NI].astype(F32)
    source_t[...], kind_t[...] = lists_across(source_v, kind_v)
    count_into(psource_t, pkind_t, 0, PROWS, pcounted_v)

    for copy in mine:
        copy.wait()
    z_copies = []
    for n, (part, waits) in enumerate(PIECES):
        for o in range(3):
            for k in waits:
                y_copies[o][k].wait_recv()
        half = own_v[part].astype(F32)
        for o in range(3):
            half = half + from_y[o, part].astype(F32)
        half_v[part] = half.astype(BF16)
        copy = remote(half_v.at[part], from_z.at[part], z_send.at[n], z_recv.at[n], z_peer)
        copy.start()
        z_copies.append(copy)
    sends += z_copies
    count_windows(0, WINDOWS)
    for copy in weights:
        copy.wait()

    n_copies = []
    for n, (part, _) in enumerate(PIECES):
        z_copies[n].wait_recv()
        near_v[0, part] = (half_v[part].astype(F32) + from_z[part].astype(F32)).astype(BF16)
        n_copies.append(
            [
                remote(
                    near_v.at[0, part],
                    near_v.at[block, part],
                    n_send.at[n * 4 + k],
                    n_recv.at[n * 4 + k],
                    device,
                )
                for k, (block, device) in enumerate(zip(blocks, partners))
            ]
        )
        for copy in n_copies[n]:
            copy.start()
        sends += n_copies[n]

    nothing = jnp.zeros((256 - REACH, NC), BF16)
    flat_ops = ops_v[...].reshape(NOPS * NC, NC)
    keep = lax.broadcasted_iota(jnp.int32, (ROWS // 2, NC), 1) < NTERMS
    l_copies = []
    for n, (part, _) in enumerate(PIECES):
        for copy in n_copies[n]:
            copy.wait_recv()
        for w in range(part.start // WINDOW, part.stop // WINDOW):
            boxes = WINDOW if w else PROWS
            at = (w - 1) * WINDOW if w else ROWS
            near = near_v[:, w * WINDOW : (w + 1) * WINDOW, :].reshape(REACH, NC)
            near = jnp.concatenate([near, nothing], axis=0)
            counted = counted_v.at[w - 1] if w else pcounted_v
            kinds = 512 // boxes
            for c in range(NOPS // kinds):
                grouped = jnp.dot(
                    counted[c * 512 : (c + 1) * 512, :], near, preferred_element_type=F32
                ).astype(BF16)
                for t in range(kinds):
                    kind = c * kinds + t
                    grouped_v[at : at + boxes, kind * NC : (kind + 1) * NC] = grouped[
                        t * boxes : (t + 1) * boxes, :
                    ]
        lo = n * (ROWS // 2)
        rows = grouped_v[lo : lo + ROWS // 2, :]
        if n == 0:
            rows = jnp.concatenate([rows, grouped_v[ROWS:, :]], axis=0)
        far = jnp.dot(rows, flat_ops, preferred_element_type=F32)
        if n == 0:
            parent_local = (coarse_v[...] + far[ROWS // 2 :, :]).astype(BF16)
            for octant in range(8):
                spread_v[pl.ds(octant, PROWS, stride=8), :] = jnp.dot(
                    parent_local, shift_v[octant], preferred_element_type=F32
                )
        whole = spread_v[lo : lo + ROWS // 2, :] + far[: ROWS // 2, :]
        here = pl.ds(pl.multiple_of(row0 + lo, ROWS // 2), ROWS // 2)
        local_v[here, :] = jnp.where(keep, whole, 0.0).astype(BF16)
        l_copies.append(
            [
                remote(
                    local_v.at[here], local_v.at[here], l_send.at[n * 3 + o], l_recv.at[n * 3 + o], device
                )
                for o, device in enumerate(y_peers)
            ]
        )
        for o in (1, 0, 2):
            l_copies[n][o].start()
        sends += l_copies[n]

    lane = lax.broadcasted_iota(jnp.int32, (16, ROWS), 1)

    def evaluate(start):
        local = local_v[pl.ds(start, ROWS), :]
        found = jnp.zeros((16, ROWS), F32)
        for c in range(ROWS // 32):
            slots = basis_v[pl.ds(start + c * 32, 32)].reshape(32 * 16, NC)
            values = lax.dot_general(
                slots, local, (((1,), (1,)), ((), ())), preferred_element_type=F32
            )
            for b in range(32):
                found = jnp.where(lane == c * 32 + b, values[b * 16 : (b + 1) * 16, :], found)
        out[:, pl.ds(start, ROWS)] = found

    evaluate(row0)
    for o in (0, 2, 1):
        for n in range(2):
            l_copies[n][o].wait_recv()
        evaluate(pl.multiple_of(((y + 3 - o) % 4) * ROWS, ROWS))
    for copy in sends:
        copy.wait_send()


def body(
    fine_parts,
    parent_parts,
    coarse_local,
    fine_source,
    fine_operator,
    parent_source,
    parent_operator,
    operators,
    child_shift,
    basis,
    counts,
):
    boxes, slots, _ = basis.shape
    vmem = pltpu.VMEM
    dma = pltpu.SemaphoreType.DMA
    values = pl.pallas_call(
        kernel,
        out_shape=jax.ShapeDtypeStruct((slots, boxes), F32),
        in_specs=[pl.BlockSpec(memory_space=pl.ANY)] * 10,
        out_specs=pl.BlockSpec(memory_space=pltpu.VMEM),
        scratch_shapes=[
            vmem((256, ROWS), jnp.int32),
            vmem((256, ROWS), jnp.int32),
            vmem((PROWS, NI), jnp.int32),
            vmem((PROWS, NI), jnp.int32),
            vmem((ROWS, 256), F32),
            vmem((ROWS, 256), F32),
            vmem((PROWS, 256), F32),
            vmem((PROWS, 256), F32),
            vmem((REACH, 256), BF16),
            vmem((MESSAGE, NC), BF16),
            vmem((PROWS, NC), F32),
            vmem((NOPS, NC, NC), BF16),
            vmem((8, NC, NC), BF16),
            vmem((boxes, slots, NC), BF16),
            vmem((2, NOPS * (WINDOW + 1), 128), F32),
            vmem((WINDOWS, NOPS * WINDOW, 256), BF16),
            vmem((NOPS * PROWS, 256), BF16),
            vmem((3, MESSAGE, NC), BF16),
            vmem((MESSAGE, NC), BF16),
            vmem((MESSAGE, NC), BF16),
            vmem((5, MESSAGE, NC), BF16),
            vmem((ROWS + PROWS, NOPS * NC), BF16),
            vmem((ROWS, NC), F32),
            vmem((boxes, NC), BF16),
            dma((10,)),
            dma((9,)),
            dma((9,)),
            dma((2,)),
            dma((2,)),
            dma((8,)),
            dma((8,)),
            dma((6,)),
            dma((6,)),
        ],
        compiler_params=pltpu.CompilerParams(
            collective_id=0, has_side_effects=True, vmem_limit_bytes=61 * 1024 * 1024
        ),
    )(
        fine_parts,
        parent_parts,
        coarse_local,
        fine_source,
        fine_operator,
        parent_source.T,
        parent_operator.T,
        operators,
        child_shift,
        basis,
    )
    slot_index = lax.iota(jnp.int32, slots)[:, None]
    return jnp.where(slot_index < counts, values, 0.0)


def solution(mesh):
    placed = (
        P("batch", "space", None),
        P("batch", "space", None),
        P("space", None),
        P(None, "space"),
        P(None, "space"),
        P(None, "space"),
        P(None, "space"),
        P(),
        P(),
        P("space", "batch", None),
        P("batch", "space"),
    )
    return jax.shard_map(
        body, mesh=mesh, in_specs=placed, out_specs=P("batch", "space"), check_vma=False
    )
```

time: 49.8 us -> 38.5 us (0.77)
  local copies, waits for them, and re-layouts: 10.4 us -> 0.01 us
  Pallas kernels: 38.2 us -> 36.9 us
  other arithmetic: 0.62 us -> 1.38 us
    unnamed x20 -> x2, local copies, waits for them, and re-layouts: 10.4 us -> 0.01 us
    pallas_call x1, Pallas kernels: 38.2 us -> 36.9 us  [body(): pl.pallas_call(kernel, out_shape=jax.ShapeDtypeStruct((slots, boxes), F32...]
    select_n x1, other arithmetic: 0.62 us -> 1.38 us  [body(): return jnp.where(slot_index < counts, values, 0.0)]
where the time goes in v2:
time: 38.5 us; the launch traced here: 38.3 us
  Pallas kernels  36.9 us (96%)
  other arithmetic  1.38 us (4%)
    pallas_call x1, Pallas kernels, body(): pl.pallas_call(kernel, out_shape=jax.ShapeDtypeStruct((slots, boxes), F32...  36.9 us
    select_n x1, other arithmetic, body(): return jnp.where(slot_index < counts, values, 0.0)  1.38 us

profile of v2, /device:TPU:8, one launch (start us, length us, event | category | flops | bytes accessed | tf_op | source)
XLA Modules:
  0.0 38.3 jit_solution(7042498445784397564)
XLA Ops:
  0.0 0.0 copy-start
  0.0 36.9 %shard_map.109 = f32[16,512]{1,0:T(8,128)} custom-call(bf16[1,512,128]{2,1,0:T(8,128)(2,1)} %fine_parts.1, bf16[1,64,128]{2,1,0:T(8,128)(2,1)} %parent_parts.1, f32[64,128]{1,0:T(8,128)} %coarse.1, s32[189,512]{1,0:T(8,128)} %fine_source.1, s32[189,512]{1,0:T(8,128)} %fine_operator.1, s32[64,189]{1,0:T(8,128)} %bitcast.3, s32[64,189]{1,0:T(8,128)} %bitcast.4, ...), custom_call_target="tpu_custom_call" | custom-call | tf_op jit(solution)/shard_map/pallas_call | solution.py:346
  36.9 0.0 copy-done
  36.9 1.4 %fusion = f32[16,512]{1,0:T(8,128)} fusion(f32[16,512]{1,0:T(8,128)} %shard_map.109, s32[512]{0:T(512)S(1)} %bitcast.5), kind=kLoop, calls=%fused_computation.1 | loop fusion | flops 16384 | bytes 67584 | tf_op jit(solution)/shard_map/jit(_where)/select_n | solution.py:402
Async XLA Ops:
  0.0 36.9 %copy-start = (s32[1,512]{1,0:T(1,128)S(1)}, s32[1,512]{1,0:T(1,128)}, u32[]{:S(2)}) copy-start(s32[1,512]{1,0:T(1,128)} %param.21) | copy-start | bytes 6148

commit v3 on v2

--- a/solution.py
+++ b/solution.py
@@ -19,6 +19,7 @@
 MESSAGE = WINDOW + ROWS
 FIRST = 3 * WINDOW
 PIECES = ((slice(0, FIRST), (0, 1)), (slice(FIRST, MESSAGE), (2,)))
+EARLY = 3
 MESH = pl.DeviceIdType.MESH
 F32 = jnp.float32
 BF16 = jnp.bfloat16
@@ -78,6 +79,7 @@
     operators,
     child_shift,
     basis,
+    counts,
     out,
     source_v,
     kind_v,
@@ -103,6 +105,9 @@
     grouped_v,
     spread_v,
     local_v,
+    counts_v,
+    stage_v,
+    pstage_v,
     load_sem,
     y_send,
     y_recv,
@@ -135,6 +140,7 @@
         load(parent_parts.at[0, pl.ds(pwin0, WINDOW)], own_v.at[pl.ds(0, WINDOW)], 4),
         load(fine_parts.at[0, pl.ds(row0, ROWS)], own_v.at[pl.ds(WINDOW, ROWS)], 5),
     ]
+    staged = [load(parent_parts.at[0], pstage_v, 10), load(fine_parts.at[0], stage_v, 11)]
     lists = [
         load(fine_source.at[:, pl.ds(row0, ROWS)], source_v.at[pl.ds(0, NI)], 0),
         load(fine_operator.at[:, pl.ds(row0, ROWS)], kind_v.at[pl.ds(0, NI)], 1),
@@ -168,17 +174,35 @@
 
         lax.fori_loop(first, last, window, 0)
 
+    def prepare():
+        iota_v[...] = lax.broadcasted_iota(jnp.int32, (REACH, 256), 0).astype(F32).astype(BF16)
+        for copy in lists:
+            copy.wait()
+        for lists_v, across in ((psource_v, psource_t), (pkind_v, pkind_t)):
+            across[:, 128:256] = jnp.full((PROWS, 128), 255.0, F32)
+            across[:, 0:128] = lists_v[:, 0:128].astype(F32)
+            across[:, 128:NI] = lists_v[:, 128:NI].astype(F32)
+        source_t[...], kind_t[...] = lists_across(source_v, kind_v)
+        count_into(psource_t, pkind_t, 0, PROWS, pcounted_v)
+
+    @pl.when(h == 0)
+    def _():
+        prepare()
+        count_windows(0, EARLY)
+
     await_greetings(everyone)
+    for copy in staged:
+        copy.wait()
     y_copies = []
     for o, device in enumerate(y_peers):
         there = (y + o + 1) % 4
         theirs = pl.multiple_of(there * ROWS, ROWS)
         theirs_p = pl.multiple_of((there // 2) * WINDOW, WINDOW)
         parts = (
-            (parent_parts.at[0, pl.ds(theirs_p, WINDOW)], 0, WINDOW),
-            (fine_parts.at[0, pl.ds(theirs, FIRST - WINDOW)], WINDOW, FIRST - WINDOW),
+            (pstage_v.at[pl.ds(theirs_p, WINDOW)], 0, WINDOW),
+            (stage_v.at[pl.ds(theirs, FIRST - WINDOW)], WINDOW, FIRST - WINDOW),
             (
-                fine_parts.at[0, pl.ds(theirs + FIRST - WINDOW, MESSAGE - FIRST)],
+                stage_v.at[pl.ds(theirs + FIRST - WINDOW, MESSAGE - FIRST)],
                 FIRST,
                 MESSAGE - FIRST,
             ),
@@ -203,18 +227,11 @@
         load(operators, ops_v, 7),
         load(child_shift, shift_v, 8),
         load(basis, basis_v, 9),
+        load(counts, counts_v, 12),
     ]
     sends = [copy for copies in y_copies for copy in copies]
 
-    iota_v[...] = lax.broadcasted_iota(jnp.int32, (REACH, 256), 0).astype(F32).astype(BF16)
-    for copy in lists:
-        copy.wait()
-    for lists_v, across in ((psource_v, psource_t), (pkind_v, pkind_t)):
-        across[:, 128:256] = jnp.full((PROWS, 128), 255.0, F32)
-        across[:, 0:128] = lists_v[:, 0:128].astype(F32)
-        across[:, 128:NI] = lists_v[:, 128:NI].astype(F32)
-    source_t[...], kind_t[...] = lists_across(source_v, kind_v)
-    count_into(psource_t, pkind_t, 0, PROWS, pcounted_v)
+    pl.when(h == 1)(prepare)
 
     for copy in mine:
         copy.wait()
@@ -231,7 +248,7 @@
         copy.start()
         z_copies.append(copy)
     sends += z_copies
-    count_windows(0, WINDOWS)
+    count_windows(jnp.where(h == 0, EARLY, 0), WINDOWS)
     for copy in weights:
         copy.wait()
 
@@ -316,7 +333,8 @@
             )
             for b in range(32):
                 found = jnp.where(lane == c * 32 + b, values[b * 16 : (b + 1) * 16, :], found)
-        out[:, pl.ds(start, ROWS)] = found
+        slot = lax.broadcasted_iota(jnp.int32, (16, ROWS), 0)
+        out[:, pl.ds(start, ROWS)] = jnp.where(slot < counts_v[:, pl.ds(start, ROWS)], found, 0.0)
 
     evaluate(row0)
     for o in (0, 2, 1):
@@ -343,10 +361,10 @@
     boxes, slots, _ = basis.shape
     vmem = pltpu.VMEM
     dma = pltpu.SemaphoreType.DMA
-    values = pl.pallas_call(
+    return pl.pallas_call(
         kernel,
         out_shape=jax.ShapeDtypeStruct((slots, boxes), F32),
-        in_specs=[pl.BlockSpec(memory_space=pl.ANY)] * 10,
+        in_specs=[pl.BlockSpec(memory_space=pl.ANY)] * 11,
         out_specs=pl.BlockSpec(memory_space=pltpu.VMEM),
         scratch_shapes=[
             vmem((256, ROWS), jnp.int32),
@@ -373,7 +391,10 @@
             vmem((ROWS + PROWS, NOPS * NC), BF16),
             vmem((ROWS, NC), F32),
             vmem((boxes, NC), BF16),
-            dma((10,)),
+            vmem((1, boxes), jnp.int32),
+            vmem((boxes, NC), BF16),
+            vmem((64, NC), BF16),
+            dma((13,)),
             dma((9,)),
             dma((9,)),
             dma((2,)),
@@ -397,9 +418,8 @@
         operators,
         child_shift,
         basis,
+        counts,
     )
-    slot_index = lax.iota(jnp.int32, slots)[:, None]
-    return jnp.where(slot_index < counts, values, 0.0)
 
 
 def solution(mesh):

time: 38.5 us -> 37.1 us (0.964)
  the two profiles are of different devices: /device:TPU:8 before, /device:TPU:32 now
where the time goes in v3:
time: 37.1 us; the launch traced here: 36.9 us
  Pallas kernels  35.5 us (96%)
  local copies, waits for them, and re-layouts  1.38 us (4%)
    pallas_call x1, Pallas kernels, body(): pl.pallas_call(kernel, out_shape=jax.ShapeDtypeStruct((slots, boxes), F32...  35.5 us
    unnamed x1, local copies, waits for them, and re-layouts  1.38 us

profile of v3, /device:TPU:32, one launch (start us, length us, event | category | flops | bytes accessed | tf_op | source)
XLA Modules:
  0.0 36.9 jit_solution(919569334948607263)
XLA Ops:
  0.0 35.5 %shard_map.109 = f32[16,512]{1,0:T(8,128)} custom-call(bf16[1,512,128]{2,1,0:T(8,128)(2,1)} %fine_parts.1, bf16[1,64,128]{2,1,0:T(8,128)(2,1)} %parent_parts.1, f32[64,128]{1,0:T(8,128)} %coarse.1, s32[189,512]{1,0:T(8,128)} %fine_source.1, s32[189,512]{1,0:T(8,128)} %fine_operator.1, s32[64,189]{1,0:T(8,128)} %bitcast.2, s32[64,189]{1,0:T(8,128)} %bitcast.3, ...), custom_call_target="tpu_custom_call" | custom-call | tf_op jit(solution)/shard_map/pallas_call | solution.py:364
  35.5 1.4 %copy.13 = f32[16,512]{1,0:T(8,128)} copy(f32[16,512]{1,0:T(8,128)} %shard_map.109) | data formatting | bytes 65536

commit v4 on v3

--- a/solution.py
+++ b/solution.py
@@ -174,6 +174,9 @@
 
         lax.fori_loop(first, last, window, 0)
 
+    def count_parents():
+        count_into(psource_t, pkind_t, 0, PROWS, pcounted_v)
+
     def prepare():
         iota_v[...] = lax.broadcasted_iota(jnp.int32, (REACH, 256), 0).astype(F32).astype(BF16)
         for copy in lists:
@@ -183,11 +186,11 @@
             across[:, 0:128] = lists_v[:, 0:128].astype(F32)
             across[:, 128:NI] = lists_v[:, 128:NI].astype(F32)
         source_t[...], kind_t[...] = lists_across(source_v, kind_v)
-        count_into(psource_t, pkind_t, 0, PROWS, pcounted_v)
 
     @pl.when(h == 0)
     def _():
         prepare()
+        count_parents()
         count_windows(0, EARLY)
 
     await_greetings(everyone)
@@ -222,13 +225,6 @@
     for n in range(3):
         for o in (1, 0, 2):
             y_copies[o][n].start()
-    weights = [
-        load(coarse.at[pl.ds(prow0, PROWS)], coarse_v, 6),
-        load(operators, ops_v, 7),
-        load(child_shift, shift_v, 8),
-        load(basis, basis_v, 9),
-        load(counts, counts_v, 12),
-    ]
     sends = [copy for copies in y_copies for copy in copies]
 
     pl.when(h == 1)(prepare)
@@ -248,6 +244,14 @@
         copy.start()
         z_copies.append(copy)
     sends += z_copies
+    weights = [
+        load(coarse.at[pl.ds(prow0, PROWS)], coarse_v, 6),
+        load(operators, ops_v, 7),
+        load(child_shift, shift_v, 8),
+        load(basis, basis_v, 9),
+        load(counts, counts_v, 12),
+    ]
+    pl.when(h == 1)(count_parents)
     count_windows(jnp.where(h == 0, EARLY, 0), WINDOWS)
     for copy in weights:
         copy.wait()

time: 37.1 us -> 37.1 us (level)
  no operation moved by 1% of the time
where the time goes in v4:
time: 37.1 us; the launch traced here: 36.9 us
  Pallas kernels  35.5 us (96%)
  local copies, waits for them, and re-layouts  1.38 us (4%)
    pallas_call x1, Pallas kernels, body(): pl.pallas_call(kernel, out_shape=jax.ShapeDtypeStruct((slots, boxes), F32...  35.5 us
    unnamed x1, local copies, waits for them, and re-layouts  1.38 us

profile of v4, /device:TPU:32, one launch (start us, length us, event | category | flops | bytes accessed | tf_op | source)
XLA Modules:
  0.0 36.9 jit_solution(11378963483716217385)
XLA Ops:
  0.0 35.5 %shard_map.109 = f32[16,512]{1,0:T(8,128)} custom-call(bf16[1,512,128]{2,1,0:T(8,128)(2,1)} %fine_parts.1, bf16[1,64,128]{2,1,0:T(8,128)(2,1)} %parent_parts.1, f32[64,128]{1,0:T(8,128)} %coarse.1, s32[189,512]{1,0:T(8,128)} %fine_source.1, s32[189,512]{1,0:T(8,128)} %fine_operator.1, s32[64,189]{1,0:T(8,128)} %bitcast.2, s32[64,189]{1,0:T(8,128)} %bitcast.3, ...), custom_call_target="tpu_custom_call" | custom-call | tf_op jit(solution)/shard_map/pallas_call | solution.py:368
  35.5 1.4 %copy.13 = f32[16,512]{1,0:T(8,128)} copy(f32[16,512]{1,0:T(8,128)} %shard_map.109) | data formatting | bytes 65536
